TPU v7x, 32 devices: a whole 2x2x4 slice. The times are simulated.
32 devices in a mesh: seq: 4 (over x, core), tp: 8 (over z, y).
Axes of the slice: x: 2, y: 2, z: 4, core: 2. Of those that a mesh axis runs over, the one named last changes fastest.
Arguments:
- tokens: bfloat16 [1024, 5120], P('seq', 'tp'), may hold values from -6 to 6
- norm_gain: float32 [5120], replicated, may hold values from 0.1 to 1.9
- q_weight: bfloat16 [5120, 5120], P(None, 'tp'), may hold values from -0.078125 to 0.078125
- kv_weight: bfloat16 [5120, 2, 1024], P(None, None, 'tp'), may hold values from -0.078125 to 0.078125
- out_weight: bfloat16 [5120, 5120], P('tp'), may hold values from -0.5 to 0.5
- ctx_cache: bfloat16 [4096, 2, 1024], P('seq', None, 'tp'), may hold values from -1000 to 1000, as said below
- span_start: int32 [1], replicated, may hold values from 1024 to 4096
- finished_cache: bfloat16 [4, 4096, 2, 1024], P(None, 'seq', None, 'tp'), may hold values from -6 to 6
- block_dest: int32 [256, 1], P('seq'), may hold values from 0 to 3; in each aligned block of 64 rows (0 to 63, 64 to 127, ...) at most 32 rows name the same one
Outputs:
- attended: bfloat16 [1024, 5120], P('seq', 'tp')
- page_pool: bfloat16 [4, 8192, 2, 1024], P(None, 'seq', None, 'tp')
Inputs may be any that keep to these rules, and one draw needn't show every extreme that they name: `block_dest`: among the 64 blocks of one index of seq, no decode index is named more than 32 times, and some decode index is named exactly 32 times. `ctx_cache`: keys are stored already rotated at their positions; keys may reach some hundreds in magnitude, values lie within -6 to 6.
All inputs are finite; a program needn't handle non-finite values.
Results may differ from a plain program's by a relative error of at most 0.03.
The roundings to bfloat16 on the way count: a program that leaves them out, or rounds other values in their place, can miss the bound.
Values may be sent and summed in bfloat16 or wider, within the bound.
A program may use at most 128 MiB of HBM per device.

v0:
```python
import functools
import math

import jax
import jax.numpy as jnp
from jax import lax
from jax.experimental import pallas as pl
from jax.experimental.pallas import tpu as pltpu
from jax.sharding import PartitionSpec as P

D = 5120
HD = 128
LAYERS = 4
BLK = 16
NZ = 4

rms_eps = 1e-06
rope_base = 1000000.0
neg_fill = -1e30
MESH = pl.DeviceIdType.MESH


def layer_kernel(
    n_seq, in_vmem, tokens, gain, qw, kvw, ow, ctx, cosf, sinf, span, fin, bdc, bdr,
    att, fin_all, map_all,
    tok, wq, wkv, wo, ctxb, newb, mapb, qacc, kvacc, queries, m_s, l_s, acc_s, mixed,
    ysend, yrecv, zsend, zrecv, fin_buf,
    wsem, lsem, tz_s, tz_r, ty_s, ty_r, cx_s, cx_r, cs_s, cs_r, nx_s, nx_r, ns_s, ns_r,
    fx_s, fx_r, fs_s, fs_r, mx_s, mx_r, ms_s, ms_r, ry_s, ry_r, rz_s, rz_r, fin_d,
):
    s = lax.axis_index("seq")
    t = lax.axis_index("tp")
    z, y = t // 2, t % 2
    chip, core = s // 2, s % 2
    chips = n_seq // 2
    rows, width = tokens.shape
    heads = width // HD
    ctx_rows = ctx.shape[0]

    def z_peer(k):
        return {"tp": lax.rem(z + k, NZ) * 2 + y}

    y_peer = {"tp": z * 2 + 1 - y}
    sibling = {"seq": chip * 2 + 1 - core}

    def x_peer(k):
        return {"seq": lax.rem(chip + k, chips) * 2 + core}

    def x_source(k):
        return lax.rem(chip + chips - k, chips) * 2 + core

    def remote(src, dst, ssem, rsem, device):
        return pltpu.make_async_remote_copy(
            src_ref=src, dst_ref=dst, send_sem=ssem, recv_sem=rsem,
            device_id=device, device_id_type=MESH,
        )

    held = fin_buf if in_vmem else fin_all
    local_fin = pltpu.make_async_copy(fin, held.at[s], lsem.at[1])
    local_fin.start()

    loads = [
        pltpu.make_async_copy(qw, wq, wsem.at[0]),
        pltpu.make_async_copy(kvw, wkv, wsem.at[1]),
        pltpu.make_async_copy(ow, wo, wsem.at[2]),
    ]

    barrier = pltpu.get_barrier_semaphore()
    peers = [z_peer(k) for k in range(1, NZ)] + [y_peer, sibling]
    peers += [x_peer(k) for k in range(1, chips)]
    for peer in peers:
        pl.semaphore_signal(barrier, inc=1, device_id=peer, device_id_type=MESH)
    pl.semaphore_wait(barrier, len(peers))

    tz = [
        remote(tokens, tok.at[k], tz_s.at[k], tz_r.at[k], z_peer(k)) for k in range(1, NZ)
    ]
    ty = [remote(tokens, tok.at[NZ], ty_s.at[0], ty_r.at[0], y_peer)]
    ty[0].start()
    for c in tz:
        c.start()

    cx = [
        remote(ctx, ctxb.at[s], cx_s.at[k], cx_r.at[k], x_peer(k)) for k in range(1, chips)
    ]
    for c in cx:
        c.start()
    cs = [remote(ctx, ctxb.at[s], cs_s.at[0], cs_r.at[0], sibling)]
    cs[0].start()
    for w in loads:
        w.start()
    local_ctx = pltpu.make_async_copy(ctx, ctxb.at[s], lsem.at[0])
    local_ctx.start()

    local_fin.wait()
    fx = [
        remote(held.at[s], held.at[s], fx_s.at[k], fx_r.at[k], x_peer(k))
        for k in range(1, chips)
    ]
    for c in fx:
        c.start()
    fs = [remote(held.at[s], held.at[s], fs_s.at[0], fs_r.at[0], sibling)]
    fs[0].start()
    drains = []

    def drain(src):
        if in_vmem:
            c = pltpu.make_async_copy(held.at[src], fin_all.at[src], fin_d.at[len(drains)])
            c.start()
            drains.append(c)

    drain(s)

    blocks = bdc.shape[0]
    capacity = 2 * blocks // n_seq
    slots = n_seq * capacity
    earlier = (
        lax.broadcasted_iota(jnp.int32, (blocks, blocks), 1)
        < lax.broadcasted_iota(jnp.int32, (blocks, blocks), 0)
    )
    same = bdr[...] == bdc[...]
    rank = jnp.sum(jnp.where(earlier & same, 1.0, 0.0), axis=1, keepdims=True).astype(jnp.int32)
    slot = bdc[...] * capacity + rank
    match = slot == lax.broadcasted_iota(jnp.int32, (blocks, slots), 1)
    numbers = lax.broadcasted_iota(jnp.int32, (blocks, slots), 0).astype(jnp.float32) + 1.0
    source = jnp.sum(jnp.where(match, numbers, 0.0), axis=0, keepdims=True).astype(jnp.int32) - 1
    mapb[...] = jnp.broadcast_to(source, mapb.shape)
    mx = [
        remote(mapb, map_all.at[s], mx_s.at[k], mx_r.at[k], x_peer(k)) for k in range(1, chips)
    ]
    for c in mx:
        c.start()
    ms = [remote(mapb, map_all.at[s], ms_s.at[0], ms_r.at[0], sibling)]
    ms[0].start()
    local_map = pltpu.make_async_copy(mapb, map_all.at[s], lsem.at[2])
    local_map.start()

    tok[0] = tokens[...]

    for k in range(1, NZ):
        tz[k - 1].wait_recv()
        c = remote(tok.at[k], tok.at[NZ + k], ty_s.at[k], ty_r.at[k], y_peer)
        c.start()
        ty.append(c)
    for k in range(1, chips):
        cx[k - 1].wait_recv()
        src = x_source(k)
        c = remote(ctxb.at[src], ctxb.at[src], cs_s.at[k], cs_r.at[k], sibling)
        c.start()
        cs.append(c)
    for c in ty:
        c.wait_recv()

    def squares(k, total):
        x = tok[k].astype(jnp.float32)
        return total + jnp.sum(x * x, axis=1, keepdims=True)

    total = lax.fori_loop(0, 2 * NZ, squares, jnp.zeros((rows, 1), jnp.float32))
    scale = lax.rsqrt(total / D + rms_eps)
    qacc[...] = jnp.zeros_like(qacc)
    kvacc[...] = jnp.zeros_like(kvacc)
    loads[0].wait()
    loads[1].wait()

    def project(k, carry):
        owner = lax.rem(z + NZ - lax.rem(k, NZ), NZ) * 2 + lax.rem(y + k // NZ, 2)
        x = tok[k].astype(jnp.float32)
        normed = (x * scale * gain[owner]).astype(jnp.bfloat16)
        part = pl.ds(pl.multiple_of(owner * width, HD), width)
        kvacc[...] += jnp.dot(normed, wkv[part, :], preferred_element_type=jnp.float32)
        qacc[...] += jnp.dot(normed, wq[part, :], preferred_element_type=jnp.float32)
        return carry

    lax.fori_loop(0, 2 * NZ, project, 0)
    cosine, sine = cosf[...], sinf[...]

    def rotate(x):
        return (x * cosine + pltpu.roll(x, HD // 2, 1) * sine).astype(jnp.bfloat16)

    newb[s, :, 0:HD] = rotate(kvacc[:, 0:HD])
    newb[s, :, HD : 2 * HD] = kvacc[:, HD : 2 * HD].astype(jnp.bfloat16)
    nx = [
        remote(newb.at[s], newb.at[s], nx_s.at[k], nx_r.at[k], x_peer(k)) for k in range(1, chips)
    ]
    for c in nx:
        c.start()
    ns = [remote(newb.at[s], newb.at[s], ns_s.at[0], ns_r.at[0], sibling)]
    ns[0].start()
    for h in range(heads):
        queries[h] = rotate(qacc[:, h * HD : (h + 1) * HD])

    local_ctx.wait()
    for c in cs:
        c.wait_recv()

    factor = HD**-0.5 * math.log2(math.e)
    span_first = span[0]

    def update(state, q, keys, values, mask):
        row_max, row_total, summed = state
        scores = mask(
            lax.dot_general(
                q, keys, (((1,), (1,)), ((), ())), preferred_element_type=jnp.float32
            )
            * factor
        )
        new_max = jnp.maximum(row_max, jnp.max(scores, axis=1, keepdims=True))
        weights = jnp.exp2(scores - new_max)
        rescale = jnp.exp2(row_max - new_max)
        return (
            new_max,
            row_total * rescale + jnp.sum(weights, axis=1, keepdims=True),
            summed * rescale
            + jnp.dot(
                weights.astype(jnp.bfloat16), values, preferred_element_type=jnp.float32
            ),
        )

    def cached_head(h, carry):
        q = queries[h]

        def step(i, state):
            place = i * ctx_rows + lax.broadcasted_iota(jnp.int32, (1, ctx_rows), 1)
            bias = jnp.where(place < span_first, 0.0, neg_fill)
            return update(
                state, q, ctxb[i, :, 0:HD], ctxb[i, :, HD : 2 * HD], lambda x: x + bias
            )

        row_max, row_total, summed = lax.fori_loop(
            0,
            n_seq,
            step,
            (
                jnp.full((rows, 1), neg_fill, jnp.float32),
                jnp.zeros((rows, 1), jnp.float32),
                jnp.zeros((rows, HD), jnp.float32),
            ),
        )
        m_s[h] = row_max
        l_s[h] = row_total
        acc_s[h] = summed
        return carry

    lax.fori_loop(0, heads, cached_head, 0)

    for k in range(1, chips):
        nx[k - 1].wait_recv()
        src = x_source(k)
        c = remote(newb.at[src], newb.at[src], ns_s.at[k], ns_r.at[k], sibling)
        c.start()
        ns.append(c)
    for c in ns:
        c.wait_recv()

    group = 4 if n_seq % 4 == 0 else 1
    span_keys = group * rows

    def new_head(h, carry):
        q = queries[h]

        def step(i, state):
            block = newb[pl.ds(i * group, group)].reshape(span_keys, 2 * HD)
            place = i * span_keys + lax.broadcasted_iota(jnp.int32, (rows, span_keys), 1)
            own = s * rows + lax.broadcasted_iota(jnp.int32, (rows, span_keys), 0)
            return update(
                state,
                q,
                block[:, 0:HD],
                block[:, HD : 2 * HD],
                lambda x: jnp.where(place <= own, x, neg_fill),
            )

        row_max, row_total, summed = lax.fori_loop(
            0, n_seq // group, step, (m_s[h], l_s[h], acc_s[h])
        )
        acc_s[h] = summed / row_total
        return carry

    lax.fori_loop(0, heads, new_head, 0)
    for h in range(heads):
        mixed[:, h * HD : (h + 1) * HD] = acc_s[h].astype(jnp.bfloat16)

    loads[2].wait()

    def share(owner):
        part = pl.ds(pl.multiple_of(owner * width, HD), width)
        return jnp.dot(mixed[...], wo[:, part], preferred_element_type=jnp.float32)

    order = list(range(1, NZ)) + [0]
    ry = {}
    for k in order:
        ysend[k] = share(lax.rem(z + k, NZ) * 2 + 1 - y).astype(jnp.bfloat16)
        ry[k] = remote(ysend.at[k], yrecv.at[k], ry_s.at[k], ry_r.at[k], y_peer)
        ry[k].start()

    rz = {}
    for k in range(1, NZ):
        own = share(lax.rem(z + k, NZ) * 2 + y)
        ry[k].wait_recv()
        zsend[k] = (own + yrecv[k].astype(jnp.float32)).astype(jnp.bfloat16)
        rz[k] = remote(zsend.at[k], zrecv.at[k], rz_s.at[k], rz_r.at[k], z_peer(k))
        rz[k].start()

    for k in range(1, chips):
        src = x_source(k)
        mx[k - 1].wait_recv()
        c = remote(map_all.at[src], map_all.at[src], ms_s.at[k], ms_r.at[k], sibling)
        c.start()
        ms.append(c)
        fx[k - 1].wait_recv()
        c = remote(held.at[src], held.at[src], fs_s.at[k], fs_r.at[k], sibling)
        c.start()
        fs.append(c)
        drain(src)

    result = share(z * 2 + y)
    ry[0].wait_recv()
    result = result + yrecv[0].astype(jnp.float32)
    for k in range(1, NZ):
        rz[k].wait_recv()
        result = result + zrecv[k].astype(jnp.float32)
    att[...] = result.astype(jnp.bfloat16)

    for c in ms:
        c.wait_recv()
    for k in range(chips):
        fs[k].wait_recv()
        drain(lax.rem(chip + chips - k, chips) * 2 + 1 - core)
    for c in drains:
        c.wait()
    local_map.wait()
    for c in tz + ty + cx + cs + nx + ns + fx + fs + mx + ms + list(ry.values()) + list(rz.values()):
        c.wait_send()


def pool_kernel(n_seq, capacity, fin_all, map_all, out, zeros, held, sem, in_sem):
    me = lax.axis_index("seq")
    for source in range(n_seq):
        pltpu.make_async_copy(fin_all.at[source], held.at[source], in_sem.at[source]).start()
    zeros[...] = jnp.zeros_like(zeros)

    def place(source, carry):
        pltpu.make_async_copy(fin_all.at[source], held.at[source], in_sem.at[source]).wait()

        def inner(r, carry2):
            number = map_all[source, 0, me * capacity + r]
            target = out.at[:, pl.ds((source * capacity + r) * BLK, BLK)]

            @pl.when(number >= 0)
            def _():
                pltpu.make_async_copy(
                    held.at[source, :, pl.ds(number * BLK, BLK)], target, sem
                ).start()

            @pl.when(number < 0)
            def _():
                pltpu.make_async_copy(zeros, target, sem).start()

            return carry2

        return lax.fori_loop(0, capacity, inner, carry)

    lax.fori_loop(0, n_seq, place, 0)
    pltpu.make_async_copy(out, out, sem).wait()


def on_device(
    n_seq, n_tp,
    tokens, norm_gain, q_weight, kv_weight, out_weight, ctx_cache, span_start,
    finished_cache, block_dest,
):
    rows, width = tokens.shape
    ctx_rows = ctx_cache.shape[0]
    heads = q_weight.shape[1] // HD
    chips = n_seq // 2
    seq_place = lax.axis_index("seq")
    positions = (span_start[0] + seq_place * rows + jnp.arange(rows, dtype=jnp.int32)).astype(
        jnp.float32
    )
    half = HD // 2
    frequency = jnp.exp(
        jnp.arange(half, dtype=jnp.float32) * (-2.0 * math.log(rope_base) / HD)
    )
    angles = positions[:, None] * frequency[None, :]
    cosine, sine = jnp.cos(angles), jnp.sin(angles)
    cosf = jnp.concatenate([cosine, cosine], 1)
    sinf = jnp.concatenate([-sine, sine], 1)
    blocks = block_dest.shape[0]
    capacity = 2 * blocks // n_seq
    slots = n_seq * capacity

    in_vmem = n_seq * finished_cache.size * 2 <= 12 * 1024 * 1024
    vmem = pl.BlockSpec(memory_space=pltpu.VMEM)
    anywhere = pl.BlockSpec(memory_space=pl.ANY)
    smem = pl.BlockSpec(memory_space=pltpu.SMEM)
    bf, f32 = jnp.bfloat16, jnp.float32
    dma = pltpu.SemaphoreType.DMA
    attended, fin_all, map_all = pl.pallas_call(
        functools.partial(layer_kernel, n_seq, in_vmem),
        out_shape=(
            jax.ShapeDtypeStruct((rows, width), bf),
            jax.ShapeDtypeStruct((n_seq,) + finished_cache.shape, bf),
            jax.ShapeDtypeStruct((n_seq, 8, slots), jnp.int32),
        ),
        in_specs=[
            vmem, vmem, anywhere, anywhere, anywhere, anywhere, vmem, vmem, smem, anywhere,
            vmem, vmem,
        ],
        out_specs=(vmem, anywhere, anywhere),
        scratch_shapes=[
            pltpu.VMEM((n_tp, rows, width), bf),
            pltpu.VMEM(q_weight.shape, bf),
            pltpu.VMEM((D, 2 * HD), bf),
            pltpu.VMEM(out_weight.shape, bf),
            pltpu.VMEM((n_seq, ctx_rows, 2 * HD), bf),
            pltpu.VMEM((n_seq, rows, 2 * HD), bf),
            pltpu.VMEM((8, slots), jnp.int32),
            pltpu.VMEM((rows, width), f32),
            pltpu.VMEM((rows, 2 * HD), f32),
            pltpu.VMEM((heads, rows, HD), bf),
            pltpu.VMEM((heads, rows, 1), f32),
            pltpu.VMEM((heads, rows, 1), f32),
            pltpu.VMEM((heads, rows, HD), f32),
            pltpu.VMEM((rows, width), bf),
            pltpu.VMEM((NZ, rows, width), bf),
            pltpu.VMEM((NZ, rows, width), bf),
            pltpu.VMEM((NZ, rows, width), bf),
            pltpu.VMEM((NZ, rows, width), bf),
            pltpu.VMEM(((n_seq,) + finished_cache.shape) if in_vmem else (8, HD), bf),
            dma((3,)),
            dma((3,)),
        ]
        + [dma((NZ,))] * 4
        + [dma((chips,))] * 16
        + [dma((NZ,))] * 4
        + [dma((n_seq,))],
        compiler_params=pltpu.CompilerParams(
            collective_id=0, has_side_effects=True, vmem_limit_bytes=56 * 1024 * 1024
        ),
        name="layer",
    )(
        tokens,
        norm_gain.reshape(n_tp, 1, width),
        q_weight,
        kv_weight.reshape(D, 2 * HD),
        out_weight,
        ctx_cache.reshape(ctx_rows, 2 * HD),
        cosf,
        sinf,
        span_start,
        finished_cache,
        block_dest,
        block_dest.reshape(1, blocks),
    )
    page_pool = pl.pallas_call(
        functools.partial(pool_kernel, n_seq, capacity),
        out_shape=jax.ShapeDtypeStruct(
            (LAYERS, slots * BLK) + finished_cache.shape[2:], bf
        ),
        in_specs=[anywhere, smem],
        out_specs=anywhere,
        scratch_shapes=[
            pltpu.VMEM((LAYERS, BLK) + finished_cache.shape[2:], bf),
            pltpu.VMEM((n_seq,) + finished_cache.shape, bf),
            dma,
            dma((n_seq,)),
        ],
        compiler_params=pltpu.CompilerParams(vmem_limit_bytes=56 * 1024 * 1024),
        name="pool",
    )(fin_all, map_all)
    return (attended, page_pool)


def solution(mesh):
    return jax.shard_map(
        functools.partial(on_device, mesh.shape["seq"], mesh.shape["tp"]),
        mesh=mesh,
        in_specs=(
            P("seq", "tp"),
            P(),
            P(None, "tp"),
            P(None, None, "tp"),
            P("tp", None),
            P("seq", None, "tp"),
            P(),
            P(None, "seq", None, "tp"),
            P("seq", None),
        ),
        out_specs=(P("seq", "tp"), P(None, "seq", None, "tp")),
        check_vma=False,
    )
```

profile of v0, /device:TPU:15, one launch (start us, length us, event | category | flops | bytes accessed | tf_op | source)
XLA Modules:
  0.0 134.3 jit_solution(11925658559710956632)
XLA Ops:
  1.3 1.3 %copy.11.bdc = s32[64,1]{1,0:T(8,128)} copy(s32[64,1]{0,1:T(1,128)} %param.17) | data formatting | bytes 512 | tf_op args[8]
  2.7 0.5 fusion
  3.2 0.8 pad_maximum_fusion
  4.0 2.0 %copy.17 = bf16[128,8,2,128]{3,1,2,0:T(8,128)(2,1)} copy(bf16[128,8,2,128]{3,2,1,0:T(2,128)(2,1)} %bitcast.15) | data formatting | bytes 1048576
  6.0 3.6 %copy.16 = bf16[640,8,2,128]{3,1,2,0:T(8,128)(2,1)} copy(bf16[640,8,2,128]{3,2,1,0:T(2,128)(2,1)} %bitcast.13) | data formatting | bytes 5242880
  9.6 117.7 %layer.1 = (bf16[256,640]{1,0:T(8,128)(2,1)}, bf16[4,4,1024,2,128]{4,3,2,1,0:T(2,128)(2,1)}, s32[4,8,128]{2,1,0:T(8,128)}) custom-call(bf16[256,640]{1,0:T(8,128)(2,1)} %tokens.1, f32[8,1,640]{2,1,0:T(1,128)} %bitcast.16, bf16[5120,640]{1,0:T(8,128)(2,1)} %qw.1, bf16[5120,256]{1,0:T(8,128)(2,1)} %bitcast.12, bf16[640,5120]{1,0:T(8,128)(2,1)} %ow.1, ...), custom_call_target="tpu_custom_call" | custom-call | tf_op jit(solution)/shard_map/layer/pallas_call | solution.py:398
  127.3 0.0 copy-start
  127.3 6.2 %pool.1 = bf16[4,2048,2,128]{3,2,1,0:T(2,128)(2,1)} custom-call(bf16[4,4,1024,2,128]{4,3,2,1,0:T(2,128)(2,1)} %get-tuple-element.6.fin_all, s32[4,8,128]{2,1,0:T(8,128)} %get-tuple-element.7.map_all), custom_call_target="tpu_custom_call" | custom-call | tf_op jit(solution)/shard_map/pool/pallas_call | solution.py:455
  133.6 0.0 copy-done
  133.6 0.7 copy.20
  (2 shorter events, 0.0 us)
Async XLA Ops:
  127.3 6.3 %copy-start = (bf16[256,640]{1,0:T(8,128)(2,1)S(1)}, bf16[256,640]{1,0:T(8,128)(2,1)}, u32[]{:S(2)}) copy-start(bf16[256,640]{1,0:T(8,128)(2,1)} %get-tuple-element.15) | copy-start | bytes 983044
where the time goes:
time: 135 us; the launch traced here: 134 us
  Pallas kernels  124 us (92%)
  local copies, waits for them, and re-layouts  7.6 us (6%)
  other arithmetic  1.39 us (1%)
    pallas_call x1, Pallas kernels, on_device(): pl.pallas_call(functools.partial(layer_kernel, n_seq, in_vmem), out_shape...  118 us
    unnamed x6, local copies, waits for them, and re-layouts  7.6 us
    pallas_call x1, Pallas kernels, on_device(): pl.pallas_call(functools.partial(pool_kernel, n_seq, capacity), out_shape...  6.25 us

commit v1 on v0

--- a/solution.py
+++ b/solution.py
@@ -235,6 +235,7 @@
                 jnp.zeros((rows, 1), jnp.float32),
                 jnp.zeros((rows, HD), jnp.float32),
             ),
+            unroll=n_seq <= 4,
         )
         m_s[h] = row_max
         l_s[h] = row_total

time: 135 us -> 132 us (0.978)
  Pallas kernels: 124 us -> 120 us
    pallas_call x1, Pallas kernels: 118 us -> 114 us  [on_device(): pl.pallas_call(functools.partial(layer_kernel, n_seq, in_vmem), out_shape...]
where the time goes in v1:
time: 132 us; the launch traced here: 130 us
  Pallas kernels  120 us (91%)
  local copies, waits for them, and re-layouts  7.6 us (6%)
  other arithmetic  1.39 us (1%)
  between operations  1.33 us (1%)
    pallas_call x1, Pallas kernels, on_device(): pl.pallas_call(functools.partial(layer_kernel, n_seq, in_vmem), out_shape...  114 us
    unnamed x6, local copies, waits for them, and re-layouts  7.6 us
    pallas_call x1, Pallas kernels, on_device(): pl.pallas_call(functools.partial(pool_kernel, n_seq, capacity), out_shape...  6.25 us

profile of v1, /device:TPU:15, one launch (start us, length us, event | category | flops | bytes accessed | tf_op | source)
XLA Modules:
  0.0 130.3 jit_solution(16472139548029118413)
XLA Ops:
  1.3 1.3 %copy.11.bdc = s32[64,1]{1,0:T(8,128)} copy(s32[64,1]{0,1:T(1,128)} %param.17) | data formatting | bytes 512 | tf_op args[8]
  2.7 0.5 fusion
  3.2 0.8 pad_maximum_fusion
  4.0 2.0 %copy.17 = bf16[128,8,2,128]{3,1,2,0:T(8,128)(2,1)} copy(bf16[128,8,2,128]{3,2,1,0:T(2,128)(2,1)} %bitcast.15) | data formatting | bytes 1048576
  6.0 3.6 %copy.16 = bf16[640,8,2,128]{3,1,2,0:T(8,128)(2,1)} copy(bf16[640,8,2,128]{3,2,1,0:T(2,128)(2,1)} %bitcast.13) | data formatting | bytes 5242880
  9.6 113.7 %layer.1 = (bf16[256,640]{1,0:T(8,128)(2,1)}, bf16[4,4,1024,2,128]{4,3,2,1,0:T(2,128)(2,1)}, s32[4,8,128]{2,1,0:T(8,128)}) custom-call(bf16[256,640]{1,0:T(8,128)(2,1)} %tokens.1, f32[8,1,640]{2,1,0:T(1,128)} %bitcast.16, bf16[5120,640]{1,0:T(8,128)(2,1)} %qw.1, bf16[5120,256]{1,0:T(8,128)(2,1)} %bitcast.12, bf16[640,5120]{1,0:T(8,128)(2,1)} %ow.1, ...), custom_call_target="tpu_custom_call" | custom-call | tf_op jit(solution)/shard_map/layer/pallas_call | solution.py:399
  123.3 0.0 copy-start
  123.3 6.2 %pool.1 = bf16[4,2048,2,128]{3,2,1,0:T(2,128)(2,1)} custom-call(bf16[4,4,1024,2,128]{4,3,2,1,0:T(2,128)(2,1)} %get-tuple-element.6.fin_all, s32[4,8,128]{2,1,0:T(8,128)} %get-tuple-element.7.map_all), custom_call_target="tpu_custom_call" | custom-call | tf_op jit(solution)/shard_map/pool/pallas_call | solution.py:456
  129.5 0.0 copy-done
  129.5 0.7 copy.20
  (2 shorter events, 0.0 us)
Async XLA Ops:
  123.3 6.3 %copy-start = (bf16[256,640]{1,0:T(8,128)(2,1)S(1)}, bf16[256,640]{1,0:T(8,128)(2,1)}, u32[]{:S(2)}) copy-start(bf16[256,640]{1,0:T(8,128)(2,1)} %get-tuple-element.15) | copy-start | bytes 983044
